TPU v7x, 32 devices: a whole 2x2x4 slice. The times are simulated.
32 devices in a mesh: bins: 4 (over y, x), tiles: 8 (over z, core).
Axes of the slice: x: 2, y: 2, z: 4, core: 2. Of those that a mesh axis runs over, the one named last changes fastest.
Arguments:
- spectrum: float32 [1152, 64, 1440], P('bins', 'tiles'), as said below
- sea_mask: int32 [64, 1440], P('tiles'), may hold values 0 or 1
- ice_mask: int32 [64, 1440], P('tiles'), may hold values 0 or 1
- friction: float32 [64, 1440], P('tiles'), may hold values from 0.2 to 1
- wind_dir: float32 [64, 1440], P('tiles'), may hold values from -3.140625 to 3.140625
- ocean_owner: int32 [8, 16], P('tiles'), may hold values from 0 to 3, as said below
Outputs:
- spectrum_next: float32 [1152, 64, 1440], P('bins', 'tiles')
- stokes_drift: float32 [2, 64, 16, 90], P(None, 'tiles', 'bins')
- wave_stress: float32 [2, 64, 16, 90], P(None, 'tiles', 'bins')
Inputs may be any that keep to these rules, and one draw needn't show every extreme that they name: The spectrum is positive everywhere. `ocean_owner`: in every row each owner index appears exactly 4 times.
All inputs are finite; a program needn't handle non-finite values. No bound on the sum of `sea_mask` or of `ice_mask` on one device may be relied on, other than what follows from the above.
Results may differ from a plain program's by a relative error of at most 0.0001.
Values sent between devices are 32-bit elements; how exact they have to be, the bound alone decides.
A program may use at most 192 MiB of HBM per device.

v0:
```python
import math

import jax
import jax.numpy as jnp
from jax import lax
from jax.sharding import PartitionSpec as P

NDIR = 36
NFREQ = 32
LON_BLOCKS = 16
STEPS = 4


courant_max = 0.6
grid_step = 0.25 * math.pi / 180.0


def extended(cells, sides, width):
    for axis, dim in sides:
        count = lax.axis_size(axis)
        ends = count - 1
        head = lax.slice_in_dim(cells, 0, width, axis=dim)
        tail = lax.slice_in_dim(cells, cells.shape[dim] - width, cells.shape[dim], axis=dim)
        cells = jnp.concatenate(
            [
                lax.ppermute(tail, axis, [(i, (i + 1) % count) for i in range(ends)]),
                cells,
                lax.ppermute(head, axis, [((i + 1) % count, i) for i in range(ends)]),
            ],
            axis=dim,
        )
    return cells


def row_metric(first_row, count, lat_total):
    row_pos = (first_row + jnp.arange(count)).astype(jnp.float32)
    latitude = (row_pos - lat_total / 2 + 0.5) * grid_step
    edge_lat = (lat_total / 2 - 0.5) * grid_step
    return jnp.cos(jnp.asarray(edge_lat, jnp.float32)) / jnp.cos(latitude)


def advance(center, south_row, north_row, sea_open, courant_x, courant_y):
    west_cell = jnp.roll(center, 1, axis=2)
    east_cell = jnp.roll(center, -1, axis=2)
    result = center - jnp.maximum(courant_x, 0.0) * (center - west_cell)
    result = result - jnp.maximum(-courant_x, 0.0) * (center - east_cell)
    result = result - jnp.maximum(courant_y, 0.0) * (center - south_row)
    result = result - jnp.maximum(-courant_y, 0.0) * (center - north_row)
    return result * sea_open


def shards(spectrum, sea_mask, ice_mask, friction, wind_dir, ocean_owner):
    local_bins, lat_rows, lon_cells = spectrum.shape
    lat_total = lat_rows * lax.axis_size("tiles")
    first_row = lax.axis_index("tiles") * lat_rows
    bin_index = lax.axis_index("bins") * local_bins + jnp.arange(local_bins)
    freq_pos = (bin_index // NDIR).astype(jnp.float32)
    angles = ((bin_index % NDIR).astype(jnp.float32) + 0.5) * (2.0 * math.pi / NDIR)
    speed_ratio = jnp.power(1.1, -freq_pos)
    freq_weight = jnp.power(1.03, freq_pos - (NFREQ - 1))
    cos_dir = jnp.cos(angles)
    sin_dir = jnp.sin(angles)
    sea_open = sea_mask.astype(jnp.float32)
    courant_y = (courant_max * speed_ratio * sin_dir)[:, None, None]
    base_x = courant_max * speed_ratio * cos_dir
    spectral = spectrum * sea_open
    metric = row_metric(first_row, lat_rows, lat_total)
    courant_x = base_x[:, None, None] * metric[None, :, None]
    for sub_step in range(STEPS):
        padded = extended(spectral, (("tiles", 1),), 1)
        spectral = advance(spectral, padded[:, :-2], padded[:, 2:], sea_open, courant_x, courant_y)
    growth = (
        0.5
        * friction[None] ** 2
        * freq_weight[:, None, None]
        * jnp.maximum(jnp.cos(angles[:, None, None] - wind_dir[None]), 0.0)
    )
    source = growth * spectral
    updated = (spectral + source) * (1.0 - 0.5 * ice_mask.astype(jnp.float32))
    drift_weights = jnp.stack([freq_weight * cos_dir, freq_weight * sin_dir])
    stress_weights = jnp.stack([cos_dir, sin_dir])
    drift_terms = jnp.dot(
        drift_weights,
        updated.reshape(local_bins, -1),
        precision=lax.Precision.HIGHEST,
        preferred_element_type=jnp.float32,
    )
    stress_terms = jnp.dot(
        stress_weights,
        source.reshape(local_bins, -1),
        precision=lax.Precision.HIGHEST,
        preferred_element_type=jnp.float32,
    )
    ocean_order = jnp.argsort(ocean_owner[0], stable=True)
    block_cells = lon_cells // LON_BLOCKS
    drift_terms = jnp.take(
        drift_terms.reshape(2, lat_rows, LON_BLOCKS, block_cells), ocean_order, axis=2
    )
    stress_terms = jnp.take(
        stress_terms.reshape(2, lat_rows, LON_BLOCKS, block_cells), ocean_order, axis=2
    )
    drift_total, stress_total = lax.psum((drift_terms, stress_terms), "bins")
    owned = LON_BLOCKS // lax.axis_size("bins")
    offset = lax.axis_index("bins") * owned
    drift_out = lax.dynamic_slice_in_dim(drift_total, offset, owned, 2)
    stress_out = lax.dynamic_slice_in_dim(stress_total, offset, owned, 2)
    return (updated, drift_out, stress_out)


def solution(mesh):
    placed = (
        P("bins", "tiles", None),
        P("tiles", None),
        P("tiles", None),
        P("tiles", None),
        P("tiles", None),
        P("tiles", None),
    )
    return jax.shard_map(
        shards,
        mesh=mesh,
        in_specs=placed,
        out_specs=(
            P("bins", "tiles", None),
            P(None, "tiles", "bins", None),
            P(None, "tiles", "bins", None),
        ),
        check_vma=False,
    )
```

profile of v0, /device:TPU:8, one launch (start us, length us, event | category | flops | bytes accessed | tf_op | source)
XLA Modules:
  0.0 618.0 jit_solution(13978541415643419111)
XLA Ops:
  7.2 0.0 all-reduce.3.cloned.1.call-start
  7.2 0.8 convert_element_type.79
  8.0 0.0 copy-start.2
  8.0 18.6 %copy_multiply_fusion = f32[288,8,1440]{2,0,1:T(8,128)} fusion(f32[288,8,1440]{2,1,0:T(8,128)} %param.8, f32[8,1440]{1,0:T(8,128)S(1)} %convert_element_type.79), kind=kLoop, calls=%fused_computation.66 | loop fusion | flops 3317760 | bytes 26588160 | tf_op jit(solution)/shard_map/mul | solution.py:66
  26.6 4.1 fusion.83
  30.6 1.9 collective-permute-start
  32.6 3.9 collective-permute-start.1
  36.5 0.1 cosine_multiply_fusion
  36.5 0.1 negate_maximum_fusion
  36.6 2.0 fusion.82
  38.6 0.7 fusion.67
  39.3 0.7 fusion.65
  40.0 1.2 sort.17
  41.2 0.5 compare_and_fusion
  41.8 0.0 copy-done.1
  41.9 0.6 pad_clamp_fusion
  42.5 0.1 multiply_maximum_fusion
  42.6 20.9 %fusion.81 = (f32[288,8,1439]{2,0,1:T(8,128)}, f32[288,8,1439]{2,0,1:T(8,128)}) fusion(f32[288,8,1440]{2,0,1:T(8,128)} %copy_multiply_fusion), kind=kLoop, calls=%fused_computation.129 | loop fusion | bytes 53047296 | tf_op jit(solution)/shard_map/jit(_roll_static)/slice | solution.py:44
  63.5 0.0 collective-permute-done
  63.5 0.0 collective-permute-done.1
  63.5 29.9 %fusion.28 = f32[288,8,1440]{2,0,1:T(8,128)} fusion(f32[288,8,1440]{2,0,1:T(8,128)} %copy_multiply_fusion, f32[288,1,1440]{2,0,1:T(8,128)} %collective-permute-done.1, f32[288,1,1440]{2,0,1:T(8,128)} %collective-permute-done, f32[288,8,1439]{2,0,1:T(8,128)} %get-tuple-element.41, f32[288,8,1]{2,0,1:T(8,128)S(1)} %get-tuple-element.43, ...), kind=kLoop, calls=%fused_computation.37 | loop fusion | flops 56401920 | bytes 56468736 | tf_op jit(solution)/shard_map/mul | solution.py:49
  93.3 2.2 fusion.80
  95.6 2.0 fusion.79
  97.6 1.9 collective-permute-start.2
  99.5 3.6 collective-permute-start.3
  103.2 20.8 %fusion.78 = (f32[288,8,1439]{2,0,1:T(8,128)}, f32[288,8,1439]{2,0,1:T(8,128)}) fusion(f32[288,8,1440]{2,0,1:T(8,128)} %fusion.28), kind=kLoop, calls=%fused_computation.126 | loop fusion | bytes 53047296 | tf_op jit(solution)/shard_map/jit(_roll_static)/slice | solution.py:44
  124.0 0.0 collective-permute-done.2
  124.0 0.0 collective-permute-done.3
  124.0 29.0 %fusion.21 = f32[288,8,1440]{2,0,1:T(8,128)} fusion(f32[288,8,1440]{2,0,1:T(8,128)} %fusion.28, f32[288,1,1440]{2,0,1:T(8,128)S(1)} %collective-permute-done.3, f32[288,1,1440]{2,0,1:T(8,128)S(1)} %collective-permute-done.2, f32[288,8,1439]{2,0,1:T(8,128)} %get-tuple-element.35, f32[288,8,1]{2,0,1:T(8,128)S(1)} %get-tuple-element.37, ...), kind=kLoop, calls=%fused_computation.28 | loop fusion | flops 56401920 | bytes 56468736 | tf_op jit(solution)/shard_map/mul | solution.py:49
  153.0 2.2 fusion.77
  155.2 2.0 fusion.76
  157.3 3.0 collective-permute-start.4
  160.2 13.9 %collective-permute-start.5 = (f32[288,1,1440]{2,0,1:T(8,128)S(1)}, f32[288,1,1440]{2,0,1:T(8,128)S(1)}, u32[]{:S(2)}, u32[]{:S(2)}) collective-permute-start(f32[288,1,1440]{2,0,1:T(8,128)S(1)} %get-tuple-element.33), channel_id=1, source_target_pairs={{1,0},{2,1},{3,2},{4,3},{5,4},{6,5},{7,6},{9,8},{10,9},{11,10},{12... | collective-permute-start | bytes 4976648 | tf_op jit(solution)/shard_map/ppermute | solution.py:28
  174.1 20.6 %fusion.75 = (f32[288,8,1439]{2,0,1:T(8,128)}, f32[288,8,1439]{2,0,1:T(8,128)}) fusion(f32[288,8,1440]{2,0,1:T(8,128)} %fusion.21), kind=kLoop, calls=%fused_computation.123 | loop fusion | bytes 53047296 | tf_op jit(solution)/shard_map/jit(_roll_static)/slice | solution.py:44
  194.8 0.0 collective-permute-done.4
  194.8 0.0 collective-permute-done.5
  194.8 29.0 %fusion.14 = f32[288,8,1440]{2,0,1:T(8,128)} fusion(f32[288,8,1440]{2,0,1:T(8,128)} %fusion.21, f32[288,1,1440]{2,0,1:T(8,128)S(1)} %collective-permute-done.5, f32[288,1,1440]{2,0,1:T(8,128)S(1)} %collective-permute-done.4, f32[288,8,1439]{2,0,1:T(8,128)} %get-tuple-element.29, f32[288,8,1]{2,0,1:T(8,128)S(1)} %get-tuple-element.31, ...), kind=kLoop, calls=%fused_computation.19 | loop fusion | flops 56401920 | bytes 56468736 | tf_op jit(solution)/shard_map/mul | solution.py:49
  223.8 2.2 fusion.74
  226.0 2.0 fusion.72
  228.1 1.9 collective-permute-start.6
  230.0 0.0 copy-start
  230.0 3.8 collective-permute-start.7
  233.8 20.6 %fusion.73 = (f32[288,8,1439]{2,0,1:T(8,128)}, f32[288,8,1439]{2,0,1:T(8,128)}) fusion(f32[288,8,1440]{2,0,1:T(8,128)} %fusion.14), kind=kLoop, calls=%fused_computation.121 | loop fusion | bytes 53047296 | tf_op jit(solution)/shard_map/jit(_roll_static)/slice | solution.py:43
  254.4 0.0 collective-permute-done.6
  254.4 0.0 collective-permute-done.7
  254.5 63.5 %multiply_multiply_fusion = (f32[288,8,1440]{2,0,1:T(8,128)}, f32[288,8,1440]{2,0,1:T(8,128)}) fusion(f32[8,1440]{1,0:T(8,128)S(1)} %copy-done, f32[288]{0:T(512)S(1)} %get-tuple-element.50, f32[288]{0:T(512)S(1)} %get-tuple-element.51, f32[8,1440]{1,0:T(8,128)S(1)} %multiply_multiply_fusion.1, f32[8,1440]{1,0:T(8,128)S(1)} %convert_element_type.79, ...), kind=kLoop, calls=%fused_computation.68 | loop fusion | flops 72990720 | bytes 69834240 | tf_op jit(solution)/shard_map/mul | solution.py:78
  318.0 51.5 %add_multiply_fusion = f32[288,8,1440]{2,0,1:T(8,128)} fusion(f32[288,8,1440]{2,0,1:T(8,128)} %get-tuple-element.21, f32[8,1440]{1,0:T(8,128)S(1)} %multiply_subtract_fusion, f32[8,1440]{1,0:T(8,128)S(1)} %copy-done, f32[288]{0:T(512)S(1)} %get-tuple-element.50, f32[288]{0:T(512)S(1)} %get-tuple-element.51, f32[8,1440]{1,0:T(8,128)S(1)} %multiply_multiply_fusion.1), kind=kLoop, calls=%fused_computation.67 | loop fusion | flops 23224320 | bytes 26682624 | tf_op jit(solution)/shard_map/mul | solution.py:79
  369.5 18.5 %copy.28 = f32[288,8,1440]{2,1,0:T(8,128)} copy(f32[288,8,1440]{2,0,1:T(8,128)} %add_multiply_fusion) | data formatting | bytes 26542080
  388.0 16.6 %reshape.219 = f32[288,11520]{1,0:T(8,128)} reshape(f32[288,8,1440]{2,1,0:T(8,128)} %copy.28) | data formatting | bytes 26542080 | tf_op jit(solution)/shard_map/reshape | solution.py:84
  404.6 35.3 %dot_general.15 = f32[8,16,90,288]{2,1,0,3:T(8,128)} reshape(f32[11520,288]{0,1:T(8,128)} %bitcast.22) | data formatting | bytes 26542080 | tf_op jit(solution)/shard_map/dot_general | solution.py:82
  439.9 18.3 %copy.26 = f32[288,8,1440]{2,1,0:T(8,128)} copy(f32[288,8,1440]{2,0,1:T(8,128)} %get-tuple-element.20) | data formatting | bytes 26542080 | tf_op jit(solution)/shard_map/mul | solution.py:78
  458.1 16.7 %reshape.220 = f32[288,11520]{1,0:T(8,128)} reshape(f32[288,8,1440]{2,1,0:T(8,128)} %copy.26) | data formatting | bytes 26542080 | tf_op jit(solution)/shard_map/reshape | solution.py:90
  474.8 35.1 %dot_general.18 = f32[8,16,90,288]{2,1,0,3:T(8,128)} reshape(f32[11520,288]{0,1:T(8,128)} %bitcast.21) | data formatting | bytes 26542080 | tf_op jit(solution)/shard_map/dot_general | solution.py:88
  510.0 25.6 %fusion.2 = f32[2,8,16,90]{3,0,2,1:T(2,128)S(1)} fusion(f32[8,16,90,288]{2,1,0,3:T(8,128)} %dot_general.15, f32[1,288]{1,0:T(1,128)S(1)} %copy-done.5, f32[1,288]{1,0:T(1,128)S(1)} %copy-done.6), kind=kOutput, calls=%fused_computation.4 | convolution fusion | flops 79626816 | bytes 13365504 | tf_op jit(solution)/shard_map/dot_general | solution.py:82
  535.6 1.0 gather_fusion
  536.6 25.4 %fusion = f32[2,8,16,90]{3,0,2,1:T(2,128)S(1)} fusion(f32[8,16,90,288]{2,1,0,3:T(8,128)} %dot_general.18, f32[1,288]{1,0:T(1,128)S(1)} %copy-done.3, f32[1,288]{1,0:T(1,128)S(1)} %copy-done.4), kind=kOutput, calls=%fused_computation.2 | convolution fusion | flops 79626816 | bytes 13365504 | tf_op jit(solution)/shard_map/dot_general | solution.py:88
  562.0 0.9 gather_fusion.1
  562.8 0.9 select_bitcast_fusion
  563.7 0.0 all-reduce.3.cloned.1.call-update
  563.8 44.4 %all-reduce.3.cloned.1.call-done = (f32[2,8,16,90]{3,0,1,2:T(2,128)}, f32[2,8,16,90]{3,0,1,2:T(2,128)}) async-done(((f32[2,8,16,90]{3,0,1,2:T(2,128)}, f32[2,8,16,90]{3,0,1,2:T(2,128)}), (f32[2,8,16,90]{3,0,1,2:T(2,128)}, f32[2,8,16,90]{3,0,1,2:T(2,128)})) %all-reduce.3.cloned.1.call-update) | async-done | bytes 184336 | tf_op jit(solution)/shard_map/psum | solution.py:102
  608.1 0.8 constant_dynamic-slice_fusion
  608.9 0.6 copy.30
  609.5 0.8 constant_dynamic-slice_fusion.1
  610.3 0.6 copy.29
  (21 shorter events, 0.1 us)
Async XLA Ops:
  7.2 601.0 %all-reduce.3.cloned.1.call-start = ((), (), s32[]{:S(2)}) async-start(), calls=%async_computation | async-start | bytes 524288 | tf_op jit(solution)/shard_map/psum | solution.py:102
  8.0 32.0 %copy-start.8 = (s32[1,16]{1,0:T(1,128)S(1)}, s32[1,16]{1,0:T(1,128)}, u32[]{:S(2)}) copy-start(s32[1,16]{1,0:T(1,128)} %param.13) | copy-start | bytes 196
  8.0 33.8 %copy-start.1 = (f32[8,1440]{1,0:T(8,128)S(1)}, f32[8,1440]{1,0:T(8,128)}, u32[]{:S(2)}) copy-start(f32[8,1440]{1,0:T(8,128)} %param.11) | copy-start | bytes 138244
  8.0 33.8 %copy-start.2 = (s32[8,1440]{1,0:T(8,128)S(1)}, s32[8,1440]{1,0:T(8,128)}, u32[]{:S(2)}) copy-start(s32[8,1440]{1,0:T(8,128)} %param.10) | copy-start | bytes 138244
  30.6 32.8 %collective-permute-start = (f32[288,1,1440]{2,0,1:T(8,128)}, f32[288,1,1440]{2,0,1:T(8,128)}, u32[]{:S(2)}, u32[]{:S(2)}) collective-permute-start(f32[288,1,1440]{2,0,1:T(8,128)} %get-tuple-element.44), channel_id=1, source_target_pairs={{0,1},{1,2},{2,3},{3,4},{4,5},{5,6},{6,7},{8,9},{9,10},{10,11},{11... | collective-permute-start | bytes 4976648 | tf_op jit(solution)/shard_map/ppermute | solution.py:26
  32.6 30.9 %collective-permute-start.1 = (f32[288,1,1440]{2,0,1:T(8,128)}, f32[288,1,1440]{2,0,1:T(8,128)}, u32[]{:S(2)}, u32[]{:S(2)}) collective-permute-start(f32[288,1,1440]{2,0,1:T(8,128)} %get-tuple-element.45), channel_id=1, source_target_pairs={{1,0},{2,1},{3,2},{4,3},{5,4},{6,5},{7,6},{9,8},{10,9},{11,10},{12... | collective-permute-start | bytes 4976648 | tf_op jit(solution)/shard_map/ppermute | solution.py:28
  97.6 26.4 %collective-permute-start.2 = (f32[288,1,1440]{2,0,1:T(8,128)S(1)}, f32[288,1,1440]{2,0,1:T(8,128)S(1)}, u32[]{:S(2)}, u32[]{:S(2)}) collective-permute-start(f32[288,1,1440]{2,0,1:T(8,128)S(1)} %get-tuple-element.38), channel_id=1, source_target_pairs={{0,1},{1,2},{2,3},{3,4},{4,5},{5,6},{6,7},{8,9},{9,10},{10,11},{11... | collective-permute-start | bytes 4976648 | tf_op jit(solution)/shard_map/ppermute | solution.py:26
  99.5 24.4 %collective-permute-start.3 = (f32[288,1,1440]{2,0,1:T(8,128)S(1)}, f32[288,1,1440]{2,0,1:T(8,128)S(1)}, u32[]{:S(2)}, u32[]{:S(2)}) collective-permute-start(f32[288,1,1440]{2,0,1:T(8,128)S(1)} %get-tuple-element.39), channel_id=1, source_target_pairs={{1,0},{2,1},{3,2},{4,3},{5,4},{6,5},{7,6},{9,8},{10,9},{11,10},{12... | collective-permute-start | bytes 4976648 | tf_op jit(solution)/shard_map/ppermute | solution.py:28
  157.3 37.5 %collective-permute-start.4 = (f32[288,1,1440]{2,0,1:T(8,128)S(1)}, f32[288,1,1440]{2,0,1:T(8,128)S(1)}, u32[]{:S(2)}, u32[]{:S(2)}) collective-permute-start(f32[288,1,1440]{2,0,1:T(8,128)S(1)} %get-tuple-element.32), channel_id=1, source_target_pairs={{0,1},{1,2},{2,3},{3,4},{4,5},{5,6},{6,7},{8,9},{9,10},{10,11},{11... | collective-permute-start | bytes 4976648 | tf_op jit(solution)/shard_map/ppermute | solution.py:26
  160.2 34.6 %collective-permute-start.5 = (f32[288,1,1440]{2,0,1:T(8,128)S(1)}, f32[288,1,1440]{2,0,1:T(8,128)S(1)}, u32[]{:S(2)}, u32[]{:S(2)}) collective-permute-start(f32[288,1,1440]{2,0,1:T(8,128)S(1)} %get-tuple-element.33), channel_id=1, source_target_pairs={{1,0},{2,1},{3,2},{4,3},{5,4},{6,5},{7,6},{9,8},{10,9},{11,10},{12... | collective-permute-start | bytes 4976648 | tf_op jit(solution)/shard_map/ppermute | solution.py:28
  228.1 26.4 %collective-permute-start.6 = (f32[288,1,1440]{2,0,1:T(8,128)S(1)}, f32[288,1,1440]{2,0,1:T(8,128)}, u32[]{:S(2)}, u32[]{:S(2)}) collective-permute-start(f32[288,1,1440]{2,0,1:T(8,128)S(1)} %get-tuple-element.26), channel_id=1, source_target_pairs={{0,1},{1,2},{2,3},{3,4},{4,5},{5,6},{6,7},{8,9},{9,10},{10,11},{11... | collective-permute-start | bytes 4976648 | tf_op jit(solution)/shard_map/ppermute | solution.py:26
  230.0 24.5 %copy-start = (f32[8,1440]{1,0:T(8,128)S(1)}, f32[8,1440]{1,0:T(8,128)}, u32[]{:S(2)}) copy-start(f32[8,1440]{1,0:T(8,128)} %param.12) | copy-start | bytes 138244
  230.0 24.4 %collective-permute-start.7 = (f32[288,1,1440]{2,0,1:T(8,128)S(1)}, f32[288,1,1440]{2,0,1:T(8,128)}, u32[]{:S(2)}, u32[]{:S(2)}) collective-permute-start(f32[288,1,1440]{2,0,1:T(8,128)S(1)} %get-tuple-element.27), channel_id=1, source_target_pairs={{1,0},{2,1},{3,2},{4,3},{5,4},{6,5},{7,6},{9,8},{10,9},{11,10},{12... | collective-permute-start | bytes 4976648 | tf_op jit(solution)/shard_map/ppermute | solution.py:28
  474.8 35.1 %copy-start.5 = (f32[1,288]{1,0:T(1,128)S(1)}, f32[1,288]{1,0:T(1,128)}, u32[]{:S(2)}) copy-start(f32[1,288]{1,0:T(1,128)} %get-tuple-element.56) | copy-start | bytes 3460
  474.8 35.1 %copy-start.6 = (f32[1,288]{1,0:T(1,128)S(1)}, f32[1,288]{1,0:T(1,128)}, u32[]{:S(2)}) copy-start(f32[1,288]{1,0:T(1,128)} %get-tuple-element.57) | copy-start | bytes 3460
  509.9 26.6 %copy-start.3 = (f32[1,288]{1,0:T(1,128)S(1)}, f32[1,288]{1,0:T(1,128)}, u32[]{:S(2)}) copy-start(f32[1,288]{1,0:T(1,128)} %get-tuple-element.54) | copy-start | bytes 3460
  509.9 26.6 %copy-start.4 = (f32[1,288]{1,0:T(1,128)S(1)}, f32[1,288]{1,0:T(1,128)}, u32[]{:S(2)}) copy-start(f32[1,288]{1,0:T(1,128)} %get-tuple-element.55) | copy-start | bytes 3460
  535.6 27.3 %copy-start.7 = (pred[16]{0:T(512)(128)(4,1)S(1)}, pred[16]{0:T(512)(128)(4,1)}, u32[]{:S(2)}) copy-start(pred[16]{0:T(512)(128)(4,1)} %compare_and_fusion) | copy-start | bytes 52
Sparse Core Ops, SparseCore 0:
  563.9 44.2 all-reduce.2
where the time goes:
time: 622 us; the launch traced here: 618 us
  local copies, waits for them, and re-layouts  247 us (40%)
  other arithmetic  227 us (36%)
  matrix products  51 us (8%)
  waiting for transfers between devices  44.4 us (7%)
  starting transfers between devices  34 us (5%)
  between operations  14.5 us (2%)
    mul x3, other arithmetic, advance(): return result * sea_open  87.9 us
    slice x6, local copies, waits for them, and re-layouts, advance(): east_cell = jnp.roll(center, -1, axis=2)  68.4 us
    mul x1, other arithmetic, shards(): source = growth * spectral  63.5 us
    mul x1, other arithmetic, shards(): updated = (spectral + source) * (1.0 - 0.5 * ice_mask.astype(jnp.float32))  51.5 us
    psum x1, waiting for transfers between devices, shards(): drift_total, stress_total = lax.psum((drift_terms, stress_terms), 'bins')  44.4 us
    dot_general x1, local copies, waits for them, and re-layouts, shards(): jnp.dot(drift_weights, updated.reshape(local_bins, -1), precision=lax.Pre...  35.3 us
    dot_general x1, local copies, waits for them, and re-layouts, shards(): jnp.dot(stress_weights, source.reshape(local_bins, -1), precision=lax.Pre...  35.1 us
    dot_general x1, matrix products, shards(): jnp.dot(drift_weights, updated.reshape(local_bins, -1), precision=lax.Pre...  25.6 us
  transfers between devices with their start and end apart: 9, of which 1 were waited for; matrix products, arithmetic and copies ran while one was open for 14% of the time, Pallas kernels for 0%

commit v1 on v0

v1 whole, which is shorter than its diff:
```python
import functools
import math

import jax
import jax.numpy as jnp
import numpy as np
from jax import lax
from jax.experimental import pallas as pl
from jax.experimental.pallas import tpu as pltpu
from jax.sharding import PartitionSpec as P

NDIR = 36
QUAD = NDIR // 4
NFREQ = 32
LON_BLOCKS = 16
STEPS = 4
HALO = 4
LANES = 128
COURANT_MAX = 0.6
GRID_STEP = 0.25 * math.pi / 180.0
MESH = pl.DeviceIdType.MESH
ORDER = (0, 2, 1, 3)


def bin_table():
    freq = np.arange(NFREQ, dtype=np.float64)
    angle = (np.arange(NDIR, dtype=np.float64) + 0.5) * (2.0 * math.pi / NDIR)
    parts = [1.1 ** -freq, 1.03 ** (freq - (NFREQ - 1)), np.cos(angle), np.sin(angle)]
    return np.concatenate(parts).astype(np.float32)


def metric_table(tiles, rows):
    total = tiles * rows
    pos = np.arange(-HALO, total + HALO, dtype=np.float64)
    metric = math.cos((total / 2 - 0.5) * GRID_STEP) / np.cos((pos - total / 2 + 0.5) * GRID_STEP)
    out = np.zeros((tiles, 3, rows, LANES), np.float32)
    for t in range(tiles):
        base = t * rows + HALO
        south = metric[base - HALO:base]
        north = metric[base + rows:base + rows + HALO]
        out[t, 0] = metric[base:base + rows, None]
        out[t, 1] = np.concatenate([south, south])[:, None]
        out[t, 2] = np.concatenate([north, north])[:, None]
    return out


def kernel(dims, tab, owner, metric, sea, ice, friction, wind, spec,
           next_ref, sums_ref,
           field, sea_f, ice_f, fc_f, fs_f, acc, halo_s, snd, rcv, mask_s, mask_r,
           blk, part, gath,
           in_sem, out_sem, snd_sem, rcv_sem, msnd_sem, mrcv_sem, psnd_sem, prcv_sem):
    nk, nb, nt, width, pad = dims
    ntile = pad // LANES
    tail = width - (pad - LANES)
    owned = LON_BLOCKS // nb
    blk_cells = width // LON_BLOCKS
    me = lax.axis_index("bins")
    t = lax.axis_index("tiles")
    has_south = t > 0
    has_north = t < nt - 1

    def in_copy(k, q, h):
        rows = pl.ds((2 * k + h) * NDIR + q * QUAD, QUAD)
        return pltpu.make_async_copy(spec.at[rows], field.at[rows], in_sem.at[k, q, h])

    def out_copy(k, q, h):
        rows = pl.ds((2 * k + h) * NDIR + q * QUAD, QUAD)
        return pltpu.make_async_copy(field.at[rows], next_ref.at[rows], out_sem.at[k, q, h])

    def halo_copy(k, q):
        target = t + 1 if q < 2 else t - 1
        return pltpu.make_async_remote_copy(
            src_ref=snd.at[k, q], dst_ref=rcv.at[k, q],
            send_sem=snd_sem.at[k, q], recv_sem=rcv_sem.at[k, q],
            device_id={"tiles": target}, device_id_type=MESH)

    def mask_copy(side):
        target = t + 1 if side == 0 else t - 1
        return pltpu.make_async_remote_copy(
            src_ref=mask_s.at[side], dst_ref=mask_r.at[side],
            send_sem=msnd_sem.at[side], recv_sem=mrcv_sem.at[side],
            device_id={"tiles": target}, device_id_type=MESH)

    sends = (has_north, has_south)
    takes = (has_south, has_north)

    @pl.loop(0, nk)
    def _(k):
        for q in ORDER:
            for h in range(2):
                in_copy(k, q, h).start()

    barrier = pltpu.get_barrier_semaphore()

    @pl.when(has_south)
    def _():
        pl.semaphore_signal(barrier, inc=1, device_id={"tiles": t - 1}, device_id_type=MESH)

    @pl.when(has_north)
    def _():
        pl.semaphore_signal(barrier, inc=1, device_id={"tiles": t + 1}, device_id_type=MESH)

    for o in range(1, nb):
        pl.semaphore_signal(barrier, inc=1, device_id={"bins": lax.rem(me + o, nb)}, device_id_type=MESH)

    def widen(x):
        return jnp.concatenate([x, jnp.zeros((x.shape[0], pad - width), x.dtype)], axis=1)

    def wide(v):
        return jnp.concatenate([v] * ntile, axis=1)

    row_w = lax.broadcasted_iota(jnp.int32, (8, pad), 0)
    row_1 = lax.broadcasted_iota(jnp.int32, (8, LANES), 0)
    lane_1 = lax.broadcasted_iota(jnp.int32, (8, LANES), 1)

    open_cells = widen(sea[...].astype(jnp.float32))
    sea_f[...] = open_cells
    ice_f[...] = widen(1.0 - 0.5 * ice[...].astype(jnp.float32))
    strength = 0.5 * friction[...] * friction[...]
    fc_f[...] = widen(strength * jnp.cos(wind[...]))
    fs_f[...] = widen(strength * jnp.sin(wind[...]))
    acc[...] = jnp.zeros_like(acc)
    turned = pltpu.roll(open_cells, HALO, 0)
    mask_s[0] = jnp.where(row_w < HALO, turned, open_cells)
    mask_s[1] = jnp.where(row_w < HALO, open_cells, turned)

    for side in range(2):
        @pl.when(jnp.logical_not(takes[side]))
        def _():
            mask_r[side] = jnp.zeros((8, pad), jnp.float32)

            @pl.loop(0, nk)
            def _(k):
                for q in (2 * side, 2 * side + 1):
                    @pl.loop(0, QUAD)
                    def _(i):
                        rcv[k, q, i] = jnp.zeros((8, pad), jnp.float32)

    inner = jnp.logical_and(has_south, has_north)

    @pl.when(inner)
    def _():
        pl.semaphore_wait(barrier, nb + 1)

    @pl.when(jnp.logical_not(inner))
    def _():
        pl.semaphore_wait(barrier, nb)

    for side in range(2):
        @pl.when(sends[side])
        def _():
            mask_copy(side).start()

    @pl.loop(0, nk)
    def _(k):
        for q in ORDER:
            in_copy(k, q, 0).wait()
            in_copy(k, q, 1).wait()

            @pl.when(sends[q // 2])
            def _():
                @pl.loop(0, QUAD)
                def _(i):
                    first = 2 * k * NDIR + q * QUAD + i
                    a = widen(field[first])
                    b = widen(field[first + NDIR])
                    if q < 2:
                        slab = jnp.where(row_w < HALO, pltpu.roll(a, HALO, 0), b)
                        slab = slab * mask_s[0]
                    else:
                        slab = jnp.where(row_w < HALO, a, pltpu.roll(b, HALO, 0))
                        slab = slab * mask_s[1]
                    snd[k, q, i] = slab

                halo_copy(k, q).start()

    for side in range(2):
        @pl.when(takes[side])
        def _():
            mask_copy(side).wait_recv()

    def x_shift(cells, west):
        if west:
            moved = pltpu.roll(cells, 1, 1)
            around = pltpu.roll(cells[:, pad - LANES:], LANES - tail + 1, 1)
            head = jnp.where(lane_1 == 0, around, moved[:, :LANES])
            return jnp.concatenate([head, moved[:, LANES:]], axis=1)
        moved = pltpu.roll(cells, pad - 1, 1)
        around = pltpu.roll(cells[:, :LANES], tail - 1, 1)
        last = jnp.where(lane_1 == tail - 1, around, moved[:, pad - LANES:])
        return jnp.concatenate([moved[:, :pad - LANES], last], axis=1)

    def pair(k, q, i):
        north_going, west = q < 2, q in (0, 3)
        side = 0 if north_going else 1
        turn = 1 if north_going else 7
        d = q * QUAD + i
        first = 2 * k * NDIR + d
        j = me * (2 * nk) + 2 * k
        cos_d, sin_d = tab[2 * NFREQ + d], tab[2 * NFREQ + NDIR + d]
        abs_x = COURANT_MAX * (cos_d if west else -cos_d)
        abs_y = COURANT_MAX * (sin_d if north_going else -sin_d)
        speed = (tab[j], tab[j + 1])
        weight = (tab[NFREQ + j], tab[NFREQ + j + 1])
        ax = (speed[0] * abs_x, speed[1] * abs_x)
        by = (speed[0] * abs_y, speed[1] * abs_y)

        a_h = jnp.where(row_1 < HALO, ax[0], ax[1]) * metric[t, 1 + side]
        b_h = jnp.where(row_1 < HALO, by[0], by[1])
        c_h = wide(1.0 - b_h - a_h)
        a_h, b_h = wide(a_h), wide(b_h)
        cells = rcv[k, q, i]
        for step in range(STEPS - 1):
            upwind = b_h * pltpu.roll(cells, turn, 0) + a_h * x_shift(cells, west)
            cells = c_h * cells + mask_r[side] * upwind
            halo_s[step] = cells

        scaled, gained = None, None
        for h in range(2):
            at = HALO * h + (HALO - 1 if north_going else 0)
            am = ax[h] * metric[t, 0]
            keep = wide(1.0 - by[h] - am)
            am = wide(am)
            cells = widen(field[first + h * NDIR]) * sea_f[...]
            for step in range(STEPS):
                if step == 0:
                    edge = rcv[k, q, i, pl.ds(at, 1), :]
                else:
                    edge = halo_s[step - 1, pl.ds(at, 1), :]
                beside = jnp.where(row_w == (7 if north_going else 0), edge, cells)
                upwind = by[h] * pltpu.roll(beside, turn, 0) + am * x_shift(cells, west)
                cells = keep * cells + sea_f[...] * upwind
            growth = jnp.maximum(
                (weight[h] * cos_d) * fc_f[...] + (weight[h] * sin_d) * fs_f[...], 0.0)
            source = growth * cells
            updated = (cells + source) * ice_f[...]
            field[first + h * NDIR] = updated[:, :width]
            if h == 0:
                scaled, gained = weight[h] * updated, source
            else:
                scaled, gained = scaled + weight[h] * updated, gained + source
        acc[0] += cos_d * scaled
        acc[1] += sin_d * scaled
        acc[2] += cos_d * gained
        acc[3] += sin_d * gained

    @pl.loop(0, nk)
    def _(k):
        for q in ORDER:
            @pl.when(takes[q // 2])
            def _():
                halo_copy(k, q).wait_recv()

            @pl.loop(0, QUAD)
            def _(i):
                pair(k, q, i)

            out_copy(k, q, 0).start()
            out_copy(k, q, 1).start()

    for b in range(LON_BLOCKS):
        tile, off = divmod(b * blk_cells, LANES)
        for f in range(4):
            piece = acc[f, :, tile * LANES:(tile + 1) * LANES]
            if off:
                piece = pltpu.roll(piece, LANES - off, 1)
                if off + blk_cells > LANES:
                    more = acc[f, :, (tile + 1) * LANES:(tile + 2) * LANES]
                    piece = jnp.where(lane_1 < LANES - off, piece, pltpu.roll(more, LANES - off, 1))
            blk[b, f] = piece

    rank = []
    for b in range(LON_BLOCKS):
        mine = owner[0, b]
        before = jnp.int32(0)
        for c in range(LON_BLOCKS):
            if c < b:
                before += (owner[0, c] <= mine).astype(jnp.int32)
            elif c > b:
                before += (owner[0, c] < mine).astype(jnp.int32)
        rank.append(before)

    @pl.loop(0, nb)
    def _(g):
        @pl.loop(0, owned)
        def _(s):
            slot = g * owned + s
            total = jnp.zeros((4, 8, LANES), jnp.float32)
            for b in range(LON_BLOCKS):
                total += jnp.where(rank[b] == slot, 1.0, 0.0) * blk[b]
            part[g, s] = total

    def part_copy(o):
        peer = lax.rem(me + o, nb)
        return pltpu.make_async_remote_copy(
            src_ref=part.at[peer], dst_ref=gath.at[o - 1],
            send_sem=psnd_sem.at[o - 1], recv_sem=prcv_sem.at[o - 1],
            device_id={"bins": peer}, device_id_type=MESH)

    for o in range(1, nb):
        part_copy(o).start()
    for o in range(1, nb):
        part_copy(o).wait_recv()
    for s in range(owned):
        total = part[me, s]
        for o in range(1, nb):
            total += gath[o - 1, s]
        for f in range(4):
            sums_ref[f, s] = total[f, :, :blk_cells]

    for o in range(1, nb):
        part_copy(o).wait_send()
    for side in range(2):
        @pl.when(sends[side])
        def _():
            mask_copy(side).wait_send()

    @pl.loop(0, nk)
    def _(k):
        for q in ORDER:
            @pl.when(sends[q // 2])
            def _():
                halo_copy(k, q).wait_send()

            out_copy(k, q, 0).wait()
            out_copy(k, q, 1).wait()


def shards(nb, nt, spectrum, sea_mask, ice_mask, friction, wind_dir, ocean_owner):
    local_bins, rows, width = spectrum.shape
    nk = local_bins // NDIR // 2
    pad = -(-width // LANES) * LANES
    owned = LON_BLOCKS // nb
    blk_cells = width // LON_BLOCKS
    vmem = pl.BlockSpec(memory_space=pltpu.VMEM)
    smem = pl.BlockSpec(memory_space=pltpu.SMEM)
    hbm = pl.BlockSpec(memory_space=pl.ANY)
    updated, sums = pl.pallas_call(
        functools.partial(kernel, (nk, nb, nt, width, pad)),
        out_shape=(
            jax.ShapeDtypeStruct(spectrum.shape, jnp.float32),
            jax.ShapeDtypeStruct((4, owned, rows, blk_cells), jnp.float32),
        ),
        in_specs=[smem, smem, vmem, vmem, vmem, vmem, vmem, hbm],
        out_specs=(hbm, vmem),
        scratch_shapes=[
            pltpu.VMEM((local_bins, rows, width), jnp.float32),
            pltpu.VMEM((rows, pad), jnp.float32),
            pltpu.VMEM((rows, pad), jnp.float32),
            pltpu.VMEM((rows, pad), jnp.float32),
            pltpu.VMEM((rows, pad), jnp.float32),
            pltpu.VMEM((4, rows, pad), jnp.float32),
            pltpu.VMEM((STEPS - 1, rows, pad), jnp.float32),
            pltpu.VMEM((nk, 4, QUAD, rows, pad), jnp.float32),
            pltpu.VMEM((nk, 4, QUAD, rows, pad), jnp.float32),
            pltpu.VMEM((2, rows, pad), jnp.float32),
            pltpu.VMEM((2, rows, pad), jnp.float32),
            pltpu.VMEM((LON_BLOCKS, 4, rows, LANES), jnp.float32),
            pltpu.VMEM((nb, owned, 4, rows, LANES), jnp.float32),
            pltpu.VMEM((nb - 1, owned, 4, rows, LANES), jnp.float32),
            pltpu.SemaphoreType.DMA((nk, 4, 2)),
            pltpu.SemaphoreType.DMA((nk, 4, 2)),
            pltpu.SemaphoreType.DMA((nk, 4)),
            pltpu.SemaphoreType.DMA((nk, 4)),
            pltpu.SemaphoreType.DMA((2,)),
            pltpu.SemaphoreType.DMA((2,)),
            pltpu.SemaphoreType.DMA((nb - 1,)),
            pltpu.SemaphoreType.DMA((nb - 1,)),
        ],
        compiler_params=pltpu.CompilerParams(
            collective_id=0, has_side_effects=True, vmem_limit_bytes=44 * 1024 * 1024),
        cost_estimate=pl.CostEstimate(
            flops=60 * spectrum.size, bytes_accessed=8 * spectrum.size, transcendentals=0),
        name="wave_step",
    )(bin_table(), ocean_owner, metric_table(nt, rows), sea_mask, ice_mask, friction, wind_dir, spectrum)
    fields = jnp.transpose(sums, (0, 2, 1, 3))
    return updated, fields[:2], fields[2:]


def solution(mesh):
    placed = (
        P("bins", "tiles", None),
        P("tiles", None),
        P("tiles", None),
        P("tiles", None),
        P("tiles", None),
        P("tiles", None),
    )
    return jax.shard_map(
        functools.partial(shards, mesh.shape["bins"], mesh.shape["tiles"]),
        mesh=mesh,
        in_specs=placed,
        out_specs=(
            P("bins", "tiles", None),
            P(None, "tiles", "bins", None),
            P(None, "tiles", "bins", None),
        ),
        check_vma=False,
    )
```

time: 622 us -> 91.7 us (0.15)
  local copies, waits for them, and re-layouts: 247 us -> 18.4 us
  other arithmetic: 227 us -> 0 us
  Pallas kernels: 0 us -> 72.1 us
  matrix products: 51 us -> 0 us
  waiting for transfers between devices: 44.4 us -> 0 us
  starting transfers between devices: 34 us -> 0 us
  between operations: 14.5 us -> 0.66 us
    mul x10 -> x0, other arithmetic: 222 us -> none  [the longest x3 87.9 us: advance(): return result * sea_open]
    slice x12 -> x1, local copies, waits for them, and re-layouts: 102 us -> 0.01 us  [shards(): return (updated, fields[:2], fields[2:])]
    pallas_call x0 -> x1, Pallas kernels: none -> 72.1 us  [shards(): pl.pallas_call(functools.partial(kernel, (nk, nb, nt, width, pad)), out_s...]
    dot_general x2 -> x0, local copies, waits for them, and re-layouts: 70.3 us -> none  [the longest x1 35.3 us: shards(): jnp.dot(drift_weights, updated.reshape(local_bins, -1), precision=lax.Pre...]
    dot_general x2 -> x0, matrix products: 51 us -> none  [the longest x1 25.6 us: shards(): jnp.dot(drift_weights, updated.reshape(local_bins, -1), precision=lax.Pre...]
    psum x1 -> x0, waiting for transfers between devices: 44.4 us -> none  [shards(): drift_total, stress_total = lax.psum((drift_terms, stress_terms), 'bins')]
    ppermute x8 -> x0, starting transfers between devices: 33.9 us -> none  [the longest x4 25.2 us: extended(): lax.ppermute(head, axis, [((i + 1) % count, i) for i in range(ends)])]
    reshape x2 -> x0, local copies, waits for them, and re-layouts: 33.3 us -> none  [the longest x1 16.7 us: shards(): source.reshape(local_bins, -1)]
  transfers between devices with their start and end apart: 9 -> 0, of which waited for: 1 -> 0; matrix products, arithmetic and copies ran while one was open for 14% -> 0% of each run, Pallas kernels for 0% -> 0%
where the time goes in v1:
time: 91.7 us; the launch traced here: 91.2 us
  Pallas kernels  72.1 us (79%)
  local copies, waits for them, and re-layouts  18.4 us (20%)
    pallas_call x1, Pallas kernels, shards(): pl.pallas_call(functools.partial(kernel, (nk, nb, nt, width, pad)), out_s...  72.1 us
    unnamed x17, local copies, waits for them, and re-layouts  18.4 us

profile of v1, /device:TPU:8, one launch (start us, length us, event | category | flops | bytes accessed | tf_op | source)
XLA Modules:
  0.0 91.2 jit_solution(16745822388243766460)
XLA Ops:
  0.6 0.0 copy-start
  0.6 0.9 copy-done
  1.5 0.0 copy-start.1
  1.5 0.8 copy-done.1
  2.3 0.0 copy-start.2
  2.3 0.8 copy-done.2
  3.1 0.0 copy-start.3
  3.1 0.8 copy-done.3
  3.9 0.0 copy-start.4
  3.9 0.8 copy-done.4
  4.7 0.0 copy-start.5
  4.7 0.7 copy-done.5
  5.4 0.0 copy-start.6
  5.4 0.7 copy-done.6
  6.1 72.1 %wave_step.1 = (f32[288,8,1440]{2,1,0:T(8,128)}, f32[4,4,8,90]{3,2,1,0:T(8,128)S(1)}) custom-call(f32[136]{0:T(256)S(1)} %copy-done.5, s32[1,16]{1,0:T(1,128)S(1)} %copy-done.6, f32[8,3,8,128]{3,2,1,0:T(8,128)S(1)} %copy-done, s32[8,1440]{1,0:T(8,128)S(1)} %copy-done.1, s32[8,1440]{1,0:T(8,128)S(1)} %copy-done.2, f32[8,1440]{1,0:T(8,128)S(1)} %copy-done.3, ...), custom_call_target="tpu_custom_call" | custom-call | flops 199065600 | bytes 26542080 | tf_op jit(solution)/shard_map/wave_step/pallas_call | solution.py:338
  78.2 0.6 copy.12
  78.8 0.6 copy.11
  79.5 11.8 %copy.14 = f32[288,8,1440]{2,1,0:T(8,128)} copy(f32[288,8,1440]{2,1,0:T(8,128)} %get-tuple-element.15) | data formatting | bytes 26542080
  (1 shorter events, 0.0 us)
Async XLA Ops:
  0.6 0.9 copy-start
  1.5 0.8 copy-start.1
  2.3 0.8 copy-start.2
  3.1 0.8 copy-start.3
  3.9 0.8 copy-start.4
  4.7 0.7 copy-start.5
  5.4 0.7 copy-start.6

commit v2 on v1

--- a/solution.py
+++ b/solution.py
@@ -45,10 +45,10 @@
 
 
 def kernel(dims, tab, owner, metric, sea, ice, friction, wind, spec,
-           next_ref, sums_ref,
-           field, sea_f, ice_f, fc_f, fs_f, acc, halo_s, snd, rcv, mask_s, mask_r,
+           field, sums_ref,
+           sea_f, ice_f, fc_f, fs_f, acc, halo_s, snd, rcv, mask_s, mask_r,
            blk, part, gath,
-           in_sem, out_sem, snd_sem, rcv_sem, msnd_sem, mrcv_sem, psnd_sem, prcv_sem):
+           in_sem, snd_sem, rcv_sem, msnd_sem, mrcv_sem, psnd_sem, prcv_sem):
     nk, nb, nt, width, pad = dims
     ntile = pad // LANES
     tail = width - (pad - LANES)
@@ -62,10 +62,6 @@
     def in_copy(k, q, h):
         rows = pl.ds((2 * k + h) * NDIR + q * QUAD, QUAD)
         return pltpu.make_async_copy(spec.at[rows], field.at[rows], in_sem.at[k, q, h])
-
-    def out_copy(k, q, h):
-        rows = pl.ds((2 * k + h) * NDIR + q * QUAD, QUAD)
-        return pltpu.make_async_copy(field.at[rows], next_ref.at[rows], out_sem.at[k, q, h])
 
     def halo_copy(k, q):
         target = t + 1 if q < 2 else t - 1
@@ -255,8 +251,6 @@
             def _(i):
                 pair(k, q, i)
 
-            out_copy(k, q, 0).start()
-            out_copy(k, q, 1).start()
 
     for b in range(LON_BLOCKS):
         tile, off = divmod(b * blk_cells, LANES)
@@ -321,9 +315,6 @@
             @pl.when(sends[q // 2])
             def _():
                 halo_copy(k, q).wait_send()
-
-            out_copy(k, q, 0).wait()
-            out_copy(k, q, 1).wait()
 
 
 def shards(nb, nt, spectrum, sea_mask, ice_mask, friction, wind_dir, ocean_owner):
@@ -342,9 +333,8 @@
             jax.ShapeDtypeStruct((4, owned, rows, blk_cells), jnp.float32),
         ),
         in_specs=[smem, smem, vmem, vmem, vmem, vmem, vmem, hbm],
-        out_specs=(hbm, vmem),
+        out_specs=(vmem, vmem),
         scratch_shapes=[
-            pltpu.VMEM((local_bins, rows, width), jnp.float32),
             pltpu.VMEM((rows, pad), jnp.float32),
             pltpu.VMEM((rows, pad), jnp.float32),
             pltpu.VMEM((rows, pad), jnp.float32),
@@ -359,7 +349,6 @@
             pltpu.VMEM((nb, owned, 4, rows, LANES), jnp.float32),
             pltpu.VMEM((nb - 1, owned, 4, rows, LANES), jnp.float32),
             pltpu.SemaphoreType.DMA((nk, 4, 2)),
-            pltpu.SemaphoreType.DMA((nk, 4, 2)),
             pltpu.SemaphoreType.DMA((nk, 4)),
             pltpu.SemaphoreType.DMA((nk, 4)),
             pltpu.SemaphoreType.DMA((2,)),
@@ -368,7 +357,7 @@
             pltpu.SemaphoreType.DMA((nb - 1,)),
         ],
         compiler_params=pltpu.CompilerParams(
-            collective_id=0, has_side_effects=True, vmem_limit_bytes=44 * 1024 * 1024),
+            collective_id=0, has_side_effects=True, vmem_limit_bytes=40 * 1024 * 1024),
         cost_estimate=pl.CostEstimate(
             flops=60 * spectrum.size, bytes_accessed=8 * spectrum.size, transcendentals=0),
         name="wave_step",

time: 91.7 us -> 96.5 us (1.052)
  local copies, waits for them, and re-layouts: 18.4 us -> 23.5 us
    unnamed x17 -> x19, local copies, waits for them, and re-layouts: 18.4 us -> 23.5 us
where the time goes in v2:
time: 96.5 us; the launch traced here: 96.1 us
  Pallas kernels  72 us (75%)
  local copies, waits for them, and re-layouts  23.5 us (24%)
    pallas_call x1, Pallas kernels, shards(): pl.pallas_call(functools.partial(kernel, (nk, nb, nt, width, pad)), out_s...  72 us
    unnamed x19, local copies, waits for them, and re-layouts  23.5 us

profile of v2, /device:TPU:8, one launch (start us, length us, event | category | flops | bytes accessed | tf_op | source)
XLA Modules:
  0.0 96.1 jit_solution(9303744902046698255)
XLA Ops:
  0.6 0.0 copy-start.1
  0.6 0.9 copy-done.1
  1.5 0.0 copy-start.2
  1.5 0.8 copy-done.2
  2.3 0.0 copy-start.3
  2.3 0.8 copy-done.3
  3.1 0.0 copy-start.4
  3.1 0.8 copy-done.4
  3.9 0.0 copy-start.5
  3.9 0.8 copy-done.5
  4.7 0.0 copy-start.6
  4.7 0.7 copy-done.6
  5.4 0.0 copy-start.7
  5.4 0.7 copy-done.7
  6.1 72.0 %wave_step.1 = (f32[288,8,1440]{2,1,0:T(8,128)S(1)}, f32[4,4,8,90]{3,2,1,0:T(8,128)S(1)}) custom-call(f32[136]{0:T(256)S(1)} %copy-done.6, s32[1,16]{1,0:T(1,128)S(1)} %copy-done.7, f32[8,3,8,128]{3,2,1,0:T(8,128)S(1)} %copy-done.1, s32[8,1440]{1,0:T(8,128)S(1)} %copy-done.2, s32[8,1440]{1,0:T(8,128)S(1)} %copy-done.3, f32[8,1440]{1,0:T(8,128)S(1)} %copy-done.4, ...), custom_call_target="tpu_custom_call" | custom-call | flops 199065600 | bytes 26542080 | tf_op jit(solution)/shard_map/wave_step/pallas_call | solution.py:329
  78.0 0.0 copy-start
  78.0 5.0 %copy-done = f32[288,8,1440]{2,1,0:T(8,128)} copy-done((f32[288,8,1440]{2,1,0:T(8,128)}, f32[288,8,1440]{2,1,0:T(8,128)S(1)}, u32[]{:S(2)}) %copy-start) | copy-done | bytes 13271064
  83.1 0.6 copy.12
  83.7 0.6 copy.11
  84.3 11.8 %copy.14 = f32[288,8,1440]{2,1,0:T(8,128)} copy(f32[288,8,1440]{2,1,0:T(8,128)} %copy-done) | data formatting | bytes 26542080
  (1 shorter events, 0.0 us)
Async XLA Ops:
  0.6 0.9 copy-start.1
  1.5 0.8 copy-start.2
  2.3 0.8 copy-start.3
  3.1 0.8 copy-start.4
  3.9 0.8 copy-start.5
  4.7 0.7 copy-start.6
  5.4 0.7 copy-start.7
  78.0 5.0 %copy-start = (f32[288,8,1440]{2,1,0:T(8,128)}, f32[288,8,1440]{2,1,0:T(8,128)S(1)}, u32[]{:S(2)}) copy-start(f32[288,8,1440]{2,1,0:T(8,128)S(1)} %get-tuple-element.15) | copy-start | bytes 39813124
